TPU v7x, 128 devices: a whole 4x4x4 slice. The times are simulated.
128 devices in a mesh: dom: 4 (over x), head: 32 (over z, y, core).
Axes of the slice: x: 4, y: 4, z: 4, core: 2. Of those that a mesh axis runs over, the one named last changes fastest.
Arguments:
- tokens: bfloat16 [24, 64, 8192], P(None, 'dom', 'head'), may hold values from -6 to 6
- parents: int32 [64], replicated, may hold values from 0 to 63, as said below
- recurrent_state: float32 [64, 128, 64, 256], P('dom', 'head'), may hold values from -6 to 6
- value_history: float32 [64, 3, 8192], P('dom', None, 'head'), may hold values from -6 to 6
- mixing_history: float32 [64, 3, 2048], P('dom', None, 'head'), may hold values from -6 to 6
- input_gain: float32 [8192], P('head'), may hold values from 0.5 to 1.5
- gate_value_weight: bfloat16 [8192, 2, 8192], P(None, None, 'head'), may hold values from -0.0625 to 0.0625
- mixing_weight: bfloat16 [8192, 2048], P(None, 'head'), may hold values from -0.0625 to 0.0625
- step_weight: bfloat16 [8192, 128], P(None, 'head'), may hold values from -0.0625 to 0.0625
- value_kernel: float32 [4, 8192], P(None, 'head'), may hold values from -3 to 3
- value_offset: float32 [8192], P('head'), may hold values from -0.5 to 0.5
- mixing_kernel: float32 [4, 2048], P(None, 'head'), may hold values from -3 to 3
- mixing_offset: float32 [2048], P('head'), may hold values from -0.5 to 0.5
- step_offset: float32 [128], P('head'), may hold values from -4 to 0
- decay_log: float32 [128], P('head'), may hold values from -2 to 1.5
- skip_gain: float32 [128], P('head'), may hold values from 0.5 to 1.5
- output_gain: float32 [8192], P('head'), may hold values from 0.5 to 1.5
- output_weight: bfloat16 [8192, 8192], P('head'), may hold values from -0.0625 to 0.0625
Outputs:
- mixed: bfloat16 [24, 64, 8192], P(None, 'dom', 'head')
Inputs may be any that keep to these rules, and one draw needn't show every extreme that they name: parents comes from systematic resampling: it never falls with i, and offspring counts are very uneven, so that a particle's parent may sit several blocks of 16 particles away.
All inputs are finite; a program needn't handle non-finite values.
Results may differ from a plain program's by a relative error of at most 0.023.
Values may be sent and summed in bfloat16 or wider, within the bound.
A program may use at most 128 MiB of HBM per device.

v0:
```python
import jax
import jax.numpy as jnp
from jax import lax
from jax.sharding import PartitionSpec as P

HEADS = 128
GROUPS = 4
P_SIZE = 64


def causal_conv(previous, current, kernel, shift_bias):
    window = jnp.concatenate([jnp.moveaxis(previous, 1, 0), current], axis=0)
    length = current.shape[0]
    summed = jnp.zeros_like(current)
    for tap_index in range(kernel.shape[0]):
        summed = summed + kernel[tap_index] * window[tap_index : tap_index + length]
    return jax.nn.silu(summed + shift_bias)


def pick_rows(carried, pieces, wanted):
    counted = pieces[0].shape[0]
    inside = (wanted >= 0) & (wanted < counted)
    safe_rows = jnp.clip(wanted, 0, counted - 1)
    result = []
    for held_rows, source in zip(carried, pieces):
        taken_rows = jnp.take(source, safe_rows, axis=0)
        mask_shape = (wanted.shape[0],) + (1,) * (source.ndim - 1)
        result.append(jnp.where(inside.reshape(mask_shape), taken_rows, held_rows))
    return tuple(result)


def body(
    tokens,
    parents,
    recurrent_state,
    value_history,
    mixing_history,
    input_gain,
    gate_value_weight,
    mixing_weight,
    step_weight,
    value_kernel,
    value_offset,
    mixing_kernel,
    mixing_offset,
    step_offset,
    decay_log,
    skip_gain,
    output_gain,
    output_weight,
):
    steps_count, local_particles, local_width = tokens.shape
    local_heads, head_width, state_width = (
        recurrent_state.shape[1],
        recurrent_state.shape[2],
        recurrent_state.shape[3],
    )
    channels = local_heads * head_width
    row_count = steps_count * local_particles
    dom_index = lax.axis_index("dom")
    head_count = lax.axis_size("head")
    head_index = lax.axis_index("head")
    gathered, full_gain = (
        lax.all_gather(tokens, "head", axis=2, tiled=True),
        lax.all_gather(input_gain.astype(jnp.bfloat16), "head", axis=0, tiled=True).astype(
            input_gain.dtype
        ),
    )
    flat_tokens = gathered.astype(jnp.float32).reshape(row_count, -1)
    normed = (
        flat_tokens
        * lax.rsqrt(jnp.mean(flat_tokens * flat_tokens, axis=-1, keepdims=True) + 1e-05)
        * full_gain
    ).astype(jnp.bfloat16)
    gate_value = jnp.dot(
        normed,
        gate_value_weight.reshape(gate_value_weight.shape[0], 2 * channels),
        preferred_element_type=jnp.float32,
    ).reshape(steps_count, local_particles, 2, channels)
    mixing_raw = jnp.dot(normed, mixing_weight, preferred_element_type=jnp.float32).reshape(
        steps_count, local_particles, -1
    )
    step_raw = jnp.dot(normed, step_weight, preferred_element_type=jnp.float32).reshape(
        steps_count, local_particles, local_heads
    )
    first_child = dom_index * local_particles
    own_parents = lax.dynamic_slice_in_dim(parents, first_child, local_particles)
    initial = (
        jnp.zeros_like(recurrent_state),
        jnp.zeros_like(value_history),
        jnp.zeros_like(mixing_history),
    )
    start_state, value_prev, mixing_prev = pick_rows(
        initial,
        (
            lax.all_gather(recurrent_state.astype(jnp.bfloat16), "dom", axis=0, tiled=True).astype(
                jnp.float32
            ),
            lax.all_gather(value_history.astype(jnp.bfloat16), "dom", axis=0, tiled=True).astype(
                jnp.float32
            ),
            lax.all_gather(mixing_history.astype(jnp.bfloat16), "dom", axis=0, tiled=True).astype(
                jnp.float32
            ),
        ),
        own_parents,
    )
    value_act = causal_conv(value_prev, gate_value[:, :, 1], value_kernel, value_offset).reshape(
        steps_count, local_particles, local_heads, head_width
    )
    mixing_act = causal_conv(mixing_prev, mixing_raw, mixing_kernel, mixing_offset)
    mixing_all = lax.all_gather(mixing_act.astype(jnp.bfloat16), "head", axis=2, tiled=True).astype(
        mixing_act.dtype
    )
    per_group = head_count // GROUPS
    group_index = head_index // per_group
    input_mix = lax.dynamic_slice_in_dim(mixing_all, group_index * state_width, state_width, 2)
    output_mix = lax.dynamic_slice_in_dim(
        mixing_all, (GROUPS + group_index) * state_width, state_width, 2
    )
    step_size = jax.nn.softplus(step_raw + step_offset)
    decay = jnp.exp(-step_size * jnp.exp(decay_log))
    skip_term = skip_gain[:, None] * value_act

    def advance(state_now, inputs):
        value_now, input_now, output_now, size_now, decay_now = inputs
        state_now = (
            decay_now[:, :, None, None] * state_now
            + (size_now[:, :, None] * value_now)[..., None] * input_now[:, None, None, :]
        )
        read_out = jnp.einsum(
            "bhpn,bn->bhp", state_now, output_now, precision=lax.Precision.HIGHEST
        )
        return (state_now, read_out)

    unused_state, local_read = lax.scan(
        advance, start_state, (value_act, input_mix, output_mix, step_size, decay)
    )
    read_all = local_read + skip_term
    gated = read_all * jax.nn.silu(
        gate_value[:, :, 0].reshape(steps_count, local_particles, local_heads, head_width)
    )
    squares = jnp.sum(gated * gated, axis=(2, 3))
    selector = jnp.arange(GROUPS, dtype=jnp.int32) == group_index
    slots = jnp.where(selector, squares[..., None], 0.0)
    summed = lax.psum(slots, "head")
    group_total = jnp.sum(jnp.where(selector, summed, 0.0), axis=-1)
    square_mean = group_total / (HEADS // GROUPS * P_SIZE)
    scaled = (
        (gated * lax.rsqrt(square_mean[..., None, None] + 1e-05)).reshape(row_count, channels)
        * output_gain
    ).astype(jnp.bfloat16)
    output_terms = jnp.dot(scaled, output_weight, preferred_element_type=jnp.float32).reshape(
        steps_count, local_particles, -1
    )
    return lax.psum_scatter(
        output_terms.astype(jnp.bfloat16), "head", scatter_dimension=2, tiled=True
    )


def solution(mesh):
    return jax.shard_map(
        body,
        mesh=mesh,
        in_specs=(
            P(None, "dom", "head"),
            P(),
            P("dom", "head", None, None),
            P("dom", None, "head"),
            P("dom", None, "head"),
            P("head"),
            P(None, None, "head"),
            P(None, "head"),
            P(None, "head"),
            P(None, "head"),
            P("head"),
            P(None, "head"),
            P("head"),
            P("head"),
            P("head"),
            P("head"),
            P("head"),
            P("head", None),
        ),
        out_specs=P(None, "dom", "head"),
        check_vma=False,
    )
```

profile of v0, /device:TPU:0, one launch (start us, length us, event | category | flops | bytes accessed | tf_op | source)
XLA Modules:
  0.0 750.3 jit_solution(15983251670227247696)
XLA Ops:
  11.3 8.1 %copy.52 = bf16[1024,8,2,256]{3,1,2,0:T(8,128)(2,1)} copy(bf16[1024,8,2,256]{3,2,1,0:T(2,128)(2,1)} %bitcast.78) | data formatting | bytes 16777216
  19.4 11.5 %copy.43 = bf16[512,8192]{1,0:T(8,128)(2,1)} copy(bf16[512,8192]{0,1:T(8,128)(2,1)} %bitcast.77) | data formatting | bytes 16777216 | tf_op jit(solution)/shard_map/dot_general | solution.py:75
  30.9 25.8 %all-gather = bf16[32,1,256]{2,1,0:T(2,128)(2,1)S(1)} all-gather(bf16[1,1,256]{2,1,0:T(2,128)(2,1)S(1)} %reshape.138), channel_id=1, replica_groups=mesh['dom'=4,'head'=32] {'head'}, dimensions={0}, use_global_device_ids=true | all-gather | bytes 16896 | tf_op jit(solution)/shard_map/all_gather | solution.py:65
  56.8 12.3 %all_gather.21 = bf16[64,3,256]{2,0,1:T(8,128)(2,1)S(1)} all-gather(bf16[16,3,256]{2,0,1:T(8,128)(2,1)S(1)} %convert_element_type.52), channel_id=1, replica_groups=mesh['dom'=4,'head'=32] {'dom'}, dimensions={0}, use_global_device_ids=true | all-gather | bytes 122880 | tf_op jit(solution)/shard_map/all_gather | solution.py:99
  69.2 11.9 %all_gather.22 = bf16[64,3,64]{2,0,1:T(8,128)(2,1)S(1)} all-gather(bf16[16,3,64]{2,0,1:T(8,128)(2,1)S(1)} %convert_element_type.54), channel_id=1, replica_groups=mesh['dom'=4,'head'=32] {'dom'}, dimensions={0}, use_global_device_ids=true | all-gather | bytes 30720 | tf_op jit(solution)/shard_map/all_gather | solution.py:102
  90.7 7.9 %fusion.5 = f32[24,16,2,256]{3,1,2,0:T(8,128)S(1)} fusion(bf16[2,256,8192,1]{2,1,0,3:T(8,128)(2,1)} %bitcast.79, bf16[24,16,8192]{2,1,0:T(8,128)(2,1)} %all-gather.7.cloned.1.call-done, f32[8192]{0:T(1024)S(1)} %bitcast.82, f32[24,16]{1,0:T(8,128)S(1)} %add_rsqrt_fusion.1), kind=kOutput, calls=%fused_computation.18 | convolution fusion | flops 3233808384 | bytes 15500800 | tf_op jit(solution)/shard_map/dot_general | solution.py:75
  100.4 10.4 %multiply_exponential_fusion = (f32[24,16,4]{1,2,0:T(4,128)S(1)}, f32[24,16,4]{1,2,0:T(4,128)S(1)}) fusion(f32[4]{0:T(128)S(1)} %exp.23, f32[4]{0:T(128)S(1)} %copy-done.16, bf16[8192,4]{0,1:T(4,128)(2,1)S(1)} %copy-done.13, bf16[24,16,8192]{2,1,0:T(8,128)(2,1)} %all-gather.7.cloned.1.call-done, f32[8192]{0:T(1024)S(1)} %bitcast.83, ...), kind=kOutput, calls=%fused_computation.69 | convolution fusion | flops 37762560 | bytes 6403616 | tf_op jit(solution)/shard_map/dot_general | solution.py:83
  110.8 40.1 %all-gather.5.cloned.1.call-done = bf16[64,4,64,256]{3,2,1,0:T(8,128)(2,1)} async-done(((bf16[16,4,64,256]{3,2,1,0:T(8,128)(2,1)}), bf16[64,4,64,256]{3,2,1,0:T(8,128)(2,1)}) %all-gather.5.cloned.1.call-update) | async-done | bytes 8388624 | tf_op jit(solution)/shard_map/all_gather | solution.py:96
  150.9 11.3 %convert_element_type.47 = f32[64,4,64,256]{3,2,1,0:T(8,128)} convert(bf16[64,4,64,256]{3,2,1,0:T(8,128)(2,1)} %all-gather.5.cloned.1.call-done) | non-fusion elementwise | flops 4194304 | bytes 25165824 | tf_op jit(solution)/shard_map/convert_element_type | solution.py:96
  162.2 8.9 %gather_fusion = f32[16,4,64,256]{3,2,1,0:T(8,128)} fusion(f32[64,4,64,256]{3,2,1,0:T(8,128)} %convert_element_type.47, s32[1024]{0:T(1024)S(1)} %pad_clamp_fusion), kind=kCustom, calls=%fused_computation | custom fusion | bytes 8388672 | tf_op jit(solution)/shard_map/jit(_take)/gather | solution.py:26
  176.3 30.9 %all-gather.9.cloned.1.call-done = bf16[24,16,2048]{0,1,2:T(8,128)(2,1)} async-done(((bf16[24,16,64]{0,1,2:T(8,128)(2,1)}), bf16[24,16,2048]{0,1,2:T(8,128)(2,1)}) %all-gather.9.cloned.1.call-update) | async-done | bytes 1572880 | tf_op jit(solution)/shard_map/all_gather | solution.py:112
  218.0 306.0 %while.12 = (s32[]{:T(128)}, f32[16,4,64,256]{3,2,1,0:T(8,128)}, f32[24,16,4,64]{3,2,1,0:T(4,128)}, f32[24,16,4]{1,2,0:T(4,128)S(1)}, f32[24,16,4]{1,2,0:T(4,128...) while((s32[]{:T(128)}, f32[16,4,64,256]{3,2,1,0:T(8,128)}, ...), condition=%wide.region_2.3_spmd, body=%wide.region_1.2_spmd.sunk | while | flops 15732738 | bytes 12798585 | solution.py:136
  223.0 7.2 fusion.55
  235.7 7.2 fusion.55
  248.5 7.2 fusion.55
  261.2 7.2 fusion.55
  274.0 7.2 fusion.55
  286.7 7.2 fusion.55
  299.5 7.2 fusion.55
  312.2 7.2 fusion.55
  325.0 7.2 fusion.55
  337.7 7.2 fusion.55
  350.5 7.2 fusion.55
  363.2 7.2 fusion.55
  376.0 7.2 fusion.55
  388.7 7.2 fusion.55
  401.5 7.2 fusion.55
  414.2 7.2 fusion.55
  427.0 7.2 fusion.55
  439.7 7.2 fusion.55
  526.6 126.5 %psum.7 = f32[24,16,4]{1,2,0:T(4,128)S(1)} all-reduce(f32[24,16,4]{1,2,0:T(4,128)S(1)} %broadcast_select_fusion), channel_id=1, replica_groups=mesh['dom'=4,'head'=32] {'head'}, use_global_device_ids=true, to_apply=%region_4.5 | all-reduce | flops 1536 | bytes 12288 | tf_op jit(solution)/shard_map/psum | solution.py:146
  661.0 82.8 %reduce-scatter.2.cloned.1.call-done = bf16[24,16,256]{2,1,0:T(8,128)(2,1)} async-done(((bf16[24,16,8192]{2,1,0:T(8,128)(2,1)}), bf16[24,16,256]{2,1,0:T(8,128)(2,1)}) %reduce-scatter.2.cloned.1.call-update) | async-done | bytes 196624 | tf_op jit(solution)/shard_map/reduce_scatter | solution.py:156
  (281 shorter events, 219.4 us)
Async XLA Ops:
  6.5 80.5 %copy-start = (bf16[8192,64]{0,1:T(8,128)(2,1)S(1)}, bf16[8192,64]{0,1:T(8,128)(2,1)}, u32[]{:S(2)}) copy-start(bf16[8192,64]{0,1:T(8,128)(2,1)} %param.27) | copy-start | bytes 3145732
  6.5 76.1 %all-gather.7.cloned.1.call-start = ((), (), s32[]{:S(2)}) async-start(), calls=%async_computation.2 | async-start | bytes 6488064 | tf_op jit(solution)/shard_map/all_gather | solution.py:64
  7.3 143.7 %all-gather.5.cloned.1.call-start = ((), (), s32[]{:S(2)}) async-start(), calls=%async_computation.1 | async-start | bytes 10485760 | tf_op jit(solution)/shard_map/all_gather | solution.py:96
  11.2 196.0 %all-gather.9.cloned.1.call-start = ((), (), s32[]{:S(2)}) async-start(), calls=%async_computation.3 | async-start | bytes 8650752 | tf_op jit(solution)/shard_map/all_gather | solution.py:112
  19.4 11.5 %copy-start.14 = (f32[256]{0:T(256)S(1)}, f32[256]{0:T(256)}, u32[]{:S(2)}) copy-start(f32[256]{0:T(256)} %param.25) | copy-start | bytes 3076
  19.4 37.4 %copy-start.15 = (f32[4]{0:T(128)S(1)}, f32[4]{0:T(128)}, u32[]{:S(2)}) copy-start(f32[4]{0:T(128)} %param.34) | copy-start | bytes 52
  19.4 37.4 %copy-start.4 = (f32[16,3,256]{2,0,1:T(8,128)S(1)}, f32[16,3,256]{2,0,1:T(8,128)}, u32[]{:S(2)}) copy-start(f32[16,3,256]{2,0,1:T(8,128)} %param.23) | copy-start | bytes 147460
  19.4 49.8 %copy-start.5 = (f32[16,3,64]{2,0,1:T(8,128)S(1)}, f32[16,3,64]{2,0,1:T(8,128)}, u32[]{:S(2)}) copy-start(f32[16,3,64]{2,0,1:T(8,128)} %param.24) | copy-start | bytes 36868
  19.4 61.8 %copy-start.11 = (s32[64]{0:T(128)S(1)}, s32[64]{0:T(128)}, u32[]{:S(2)}) copy-start(s32[64]{0:T(128)} %param.21) | copy-start | bytes 772
  19.4 63.1 %copy-start.8 = (f32[4,64]{1,0:T(4,128)S(1)}, f32[4,64]{1,0:T(4,128)}, u32[]{:S(2)}) copy-start(f32[4,64]{1,0:T(4,128)} %param.31) | copy-start | bytes 3076
  19.4 63.1 %copy-start.6 = (f32[4,256]{1,0:T(4,128)S(1)}, f32[4,256]{1,0:T(4,128)}, u32[]{:S(2)}) copy-start(f32[4,256]{1,0:T(4,128)} %param.29) | copy-start | bytes 12292
  82.7 4.8 copy-start.2
  87.4 1.9 copy-start.10
  90.4 653.4 %reduce-scatter.2.cloned.1.call-start = ((), (), s32[]{:S(2)}) async-start(), calls=%async_computation.4 | async-start | bytes 6488064 | tf_op jit(solution)/shard_map/reduce_scatter | solution.py:156
  90.6 9.3 %copy-start.9 = (f32[256]{0:T(256)S(1)}, f32[256]{0:T(256)}, u32[]{:S(2)}) copy-start(f32[256]{0:T(256)} %param.30) | copy-start | bytes 3076
  90.6 9.8 %copy-start.13 = (bf16[8192,4]{0,1:T(4,128)(2,1)S(1)}, bf16[8192,4]{0,1:T(4,128)(2,1)}, u32[]{:S(2)}) copy-start(bf16[8192,4]{0,1:T(4,128)(2,1)} %param.28) | copy-start | bytes 196612
  90.6 9.8 %copy-start.16 = (f32[4]{0:T(128)S(1)}, f32[4]{0:T(128)}, u32[]{:S(2)}) copy-start(f32[4]{0:T(128)} %param.33) | copy-start | bytes 52
  218.0 306.0 %copy-start.3 = (f32[24,16,4,64]{3,2,1,0:T(4,128)S(1)}, f32[24,16,4,64]{3,2,1,0:T(4,128)}, u32[]{:S(2)}) copy-start(f32[24,16,4,64]{3,2,1,0:T(4,128)} %reshape_squeeze.3) | copy-start | bytes 1179652
  218.0 306.0 %copy-start.12 = (f32[4]{0:T(128)S(1)}, f32[4]{0:T(128)}, u32[]{:S(2)}) copy-start(f32[4]{0:T(128)} %param.35) | copy-start | bytes 52
  218.0 436.2 %copy-start.7 = (f32[256]{0:T(256)S(1)}, f32[256]{0:T(256)}, u32[]{:S(2)}) copy-start(f32[256]{0:T(256)} %param.36) | copy-start | bytes 3076
  654.2 89.6 %copy-start.1 = (bf16[8192,64]{0,1:T(8,128)(2,1)S(1)}, bf16[8192,64]{0,1:T(8,128)(2,1)}, u32[]{:S(2)}) copy-start(bf16[8192,64]{0,1:T(8,128)(2,1)} %param.27) | copy-start | bytes 3145732
Sparse Core Ops, SparseCore 0:
  9.5 57.0 all-gather.6
  68.3 82.6 all-gather.4
  153.2 53.9 all-gather.8
  661.1 82.6 reduce-scatter.1
where the time goes:
time: 753 us; the launch traced here: 750 us
  matrix products  199 us (26%)
  blocking collectives  177 us (24%)
  waiting for transfers between devices  155 us (21%)
  other arithmetic  131 us (17%)
  local copies, waits for them, and re-layouts  75.8 us (10%)
  between operations  13.5 us (2%)
    dot_general x24, matrix products, advance(): jnp.einsum('bhpn,bn->bhp', state_now, output_now, precision=lax.Precision...  172 us
    psum x1, blocking collectives, body(): summed = lax.psum(slots, 'head')  127 us
    add x24, other arithmetic, advance(): decay_now[:, :, None, None] * state_now  95.7 us
    reduce_scatter x1, waiting for transfers between devices, body(): lax.psum_scatter(output_terms.astype(jnp.bfloat16), 'head', scatter_dimen...  82.8 us
    all_gather x1, waiting for transfers between devices, body(): lax.all_gather(recurrent_state.astype(jnp.bfloat16), 'dom', axis=0, tiled...  40.1 us
    all_gather x1, waiting for transfers between devices, body(): lax.all_gather(mixing_act.astype(jnp.bfloat16), 'head', axis=2, tiled=True)  30.9 us
    all_gather x1, blocking collectives, body(): lax.all_gather(input_gain.astype(jnp.bfloat16), 'head', axis=0, tiled=True)  25.8 us
    squeeze x24, local copies, waits for them, and re-layouts, body(): lax.scan(advance, start_state, (value_act, input_mix, output_mix, step_si...  17.2 us
  transfers between devices with their start and end apart: 4, of which 3 were waited for; matrix products, arithmetic and copies ran while one was open for 10% of the time, Pallas kernels for 0%

commit v1 on v0

--- a/solution.py
+++ b/solution.py
@@ -109,9 +109,12 @@
         steps_count, local_particles, local_heads, head_width
     )
     mixing_act = causal_conv(mixing_prev, mixing_raw, mixing_kernel, mixing_offset)
-    mixing_all = lax.all_gather(mixing_act.astype(jnp.bfloat16), "head", axis=2, tiled=True).astype(
-        mixing_act.dtype
-    )
+    mixing_all = jnp.concatenate(
+        lax.all_to_all(
+            jnp.stack([mixing_act.astype(jnp.bfloat16)] * lax.axis_size("head")), "head", 0, 0
+        ),
+        axis=2,
+    ).astype(mixing_act.dtype)
     per_group = head_count // GROUPS
     group_index = head_index // per_group
     input_mix = lax.dynamic_slice_in_dim(mixing_all, group_index * state_width, state_width, 2)

time: 753 us -> 701 us (0.931)
  waiting for transfers between devices: 155 us -> 109 us
  local copies, waits for them, and re-layouts: 75.8 us -> 63.3 us
    all_gather x1 -> x0, waiting for transfers between devices: 30.9 us -> none  [body(): lax.all_gather(mixing_act.astype(jnp.bfloat16), 'head', axis=2, tiled=True)]
    squeeze x24, local copies, waits for them, and re-layouts: 17.2 us -> 0.05 us  [body(): lax.scan(advance, start_state, (value_act, input_mix, output_mix, step_si...]
    dynamic_update_slice x24, local copies, waits for them, and re-layouts: 14.9 us -> 0.43 us  [body(): lax.scan(advance, start_state, (value_act, input_mix, output_mix, step_si...]
    all_gather x1, waiting for transfers between devices: 40.1 us -> 25.9 us  [body(): lax.all_gather(recurrent_state.astype(jnp.bfloat16), 'dom', axis=0, tiled...]
    convert_element_type x1 -> x2, local copies, waits for them, and re-layouts: 0.95 us -> 12.8 us  [body(): mixing_all = jnp.concatenate(lax.all_to_all(jnp.stack([mixing_act.astype(...]
    unnamed x36 -> x38, local copies, waits for them, and re-layouts: 8.57 us -> 18 us
  transfers between devices with their start and end apart: 4 -> 4, of which waited for: 3 -> 2; matrix products, arithmetic and copies ran while one was open for 10% -> 12% of each run, Pallas kernels for 0% -> 0%
where the time goes in v1:
time: 701 us; the launch traced here: 699 us
  matrix products  198 us (28%)
  blocking collectives  178 us (25%)
  other arithmetic  129 us (18%)
  waiting for transfers between devices  109 us (16%)
  local copies, waits for them, and re-layouts  63.3 us (9%)
  between operations  13.5 us (2%)
    dot_general x24, matrix products, advance(): jnp.einsum('bhpn,bn->bhp', state_now, output_now, precision=lax.Precision...  172 us
    psum x1, blocking collectives, body(): summed = lax.psum(slots, 'head')  129 us
    add x24, other arithmetic, advance(): decay_now[:, :, None, None] * state_now  96.5 us
    reduce_scatter x1, waiting for transfers between devices, body(): lax.psum_scatter(output_terms.astype(jnp.bfloat16), 'head', scatter_dimen...  82.6 us
    all_gather x1, waiting for transfers between devices, body(): lax.all_gather(recurrent_state.astype(jnp.bfloat16), 'dom', axis=0, tiled...  25.9 us
    all_gather x1, blocking collectives, body(): lax.all_gather(input_gain.astype(jnp.bfloat16), 'head', axis=0, tiled=True)  25.9 us
    unnamed x38, local copies, waits for them, and re-layouts  18 us
  transfers between devices with their start and end apart: 4, of which 2 were waited for; matrix products, arithmetic and copies ran while one was open for 12% of the time, Pallas kernels for 0%

profile of v1, /device:TPU:0, one launch (start us, length us, event | category | flops | bytes accessed | tf_op | source)
XLA Modules:
  0.0 699.2 jit_solution(8689292305484334897)
XLA Ops:
  11.2 8.0 %copy.55 = bf16[1024,8,2,256]{3,1,2,0:T(8,128)(2,1)} copy(bf16[1024,8,2,256]{3,2,1,0:T(2,128)(2,1)} %bitcast.82) | data formatting | bytes 16777216
  19.2 11.9 %copy.48 = bf16[512,8192]{1,0:T(8,128)(2,1)} copy(bf16[512,8192]{0,1:T(8,128)(2,1)} %bitcast.81) | data formatting | bytes 16777216 | tf_op jit(solution)/shard_map/dot_general | solution.py:75
  31.2 25.9 %all-gather = bf16[32,1,256]{2,1,0:T(2,128)(2,1)S(1)} all-gather(bf16[1,1,256]{2,1,0:T(2,128)(2,1)S(1)} %reshape.145), channel_id=1, replica_groups=mesh['dom'=4,'head'=32] {'head'}, dimensions={0}, use_global_device_ids=true | all-gather | bytes 16896 | tf_op jit(solution)/shard_map/all_gather | solution.py:65
  57.2 12.1 %all_gather.18 = bf16[64,3,256]{2,0,1:T(8,128)(2,1)S(1)} all-gather(bf16[16,3,256]{2,0,1:T(8,128)(2,1)S(1)} %convert_element_type.58), channel_id=1, replica_groups=mesh['dom'=4,'head'=32] {'dom'}, dimensions={0}, use_global_device_ids=true | all-gather | bytes 122880 | tf_op jit(solution)/shard_map/all_gather | solution.py:99
  69.4 11.9 %all_gather.19 = bf16[64,3,64]{2,0,1:T(8,128)(2,1)S(1)} all-gather(bf16[16,3,64]{2,0,1:T(8,128)(2,1)S(1)} %convert_element_type.60), channel_id=1, replica_groups=mesh['dom'=4,'head'=32] {'dom'}, dimensions={0}, use_global_device_ids=true | all-gather | bytes 30720 | tf_op jit(solution)/shard_map/all_gather | solution.py:102
  104.1 7.9 %fusion.5 = f32[24,16,2,256]{3,1,2,0:T(8,128)S(1)} fusion(bf16[2,256,8192,1]{2,1,0,3:T(8,128)(2,1)} %bitcast.83, bf16[24,16,8192]{2,1,0:T(8,128)(2,1)} %all-gather.6.cloned.1.call-done, f32[8192]{0:T(1024)S(1)} %bitcast.86, f32[24,16]{1,0:T(8,128)S(1)} %add_rsqrt_fusion.1), kind=kOutput, calls=%fused_computation.18 | convolution fusion | flops 3233808384 | bytes 15500800 | tf_op jit(solution)/shard_map/dot_general | solution.py:75
  114.7 10.3 %multiply_exponential_fusion = (f32[24,16,4]{1,2,0:T(4,128)S(1)}, f32[24,16,4]{1,2,0:T(4,128)S(1)}) fusion(f32[4]{0:T(128)S(1)} %exp.23, f32[4]{0:T(128)S(1)} %copy-done.16, bf16[8192,4]{0,1:T(4,128)(2,1)S(1)} %copy-done.13, bf16[24,16,8192]{2,1,0:T(8,128)(2,1)} %all-gather.6.cloned.1.call-done, f32[8192]{0:T(1024)S(1)} %bitcast.87, ...), kind=kOutput, calls=%fused_computation.70 | convolution fusion | flops 37762560 | bytes 6403616 | tf_op jit(solution)/shard_map/dot_general | solution.py:83
  125.0 25.9 %all-gather.4.cloned.1.call-done = bf16[64,4,64,256]{3,2,1,0:T(8,128)(2,1)} async-done(((bf16[16,4,64,256]{3,2,1,0:T(8,128)(2,1)}), bf16[64,4,64,256]{3,2,1,0:T(8,128)(2,1)}) %all-gather.4.cloned.1.call-update) | async-done | bytes 8388624 | tf_op jit(solution)/shard_map/all_gather | solution.py:96
  150.9 11.3 %convert_element_type.53 = f32[64,4,64,256]{3,2,1,0:T(8,128)} convert(bf16[64,4,64,256]{3,2,1,0:T(8,128)(2,1)} %all-gather.4.cloned.1.call-done) | non-fusion elementwise | flops 4194304 | bytes 25165824 | tf_op jit(solution)/shard_map/convert_element_type | solution.py:96
  162.2 8.5 %gather_fusion = f32[16,4,64,256]{3,2,1,0:T(8,128)} fusion(f32[64,4,64,256]{3,2,1,0:T(8,128)} %convert_element_type.53, s32[1024]{0:T(1024)S(1)} %pad_clamp_fusion), kind=kCustom, calls=%fused_computation | custom fusion | bytes 8388672 | tf_op jit(solution)/shard_map/jit(_take)/gather | solution.py:26
  195.9 276.3 %while.12 = (s32[]{:T(128)}, f32[16,4,64,256]{3,2,1,0:T(8,128)}, f32[24,16,4,64]{3,2,1,0:T(4,128)S(1)}, f32[24,16,4]{1,2,0:T(4,128)S(1)}, f32[24,16,4]{1,2,0:T(4...) while((s32[]{:T(128)}, f32[16,4,64,256]{3,2,1,0:T(8,128)}, ...), condition=%wide.region_2.3_spmd, body=%wide.region_1.2_spmd.sunk | while | flops 15732738 | bytes 12814969 | solution.py:139
  200.2 7.2 %fusion.55 = f32[16,1,4,64]{3,1,2,0:T(1,128)S(1)} fusion(f32[16,4,64,256]{3,2,1,0:T(8,128)} %multiply_add_fusion.2, f32[16,256,1,1]{1,0,2,3:T(8,128)S(1)} %dynamic-slice_bitcast_fusion.9), kind=kOutput, calls=%fused_computation.5.clone.1 | convolution fusion | flops 12582912 | bytes 4227072 | tf_op jit(solution)/shard_map/while/body/eval_jaxpr/bhpn,bn->bhp/dot_general | solution.py:134
  211.7 7.2 %fusion.55 = f32[16,1,4,64]{3,1,2,0:T(1,128)S(1)} fusion(f32[16,4,64,256]{3,2,1,0:T(8,128)} %multiply_add_fusion.2, f32[16,256,1,1]{1,0,2,3:T(8,128)S(1)} %dynamic-slice_bitcast_fusion.9), kind=kOutput, calls=%fused_computation.5.clone.1 | convolution fusion | flops 12582912 | bytes 4227072 | tf_op jit(solution)/shard_map/while/body/eval_jaxpr/bhpn,bn->bhp/dot_general | solution.py:134
  223.3 7.2 %fusion.55 = f32[16,1,4,64]{3,1,2,0:T(1,128)S(1)} fusion(f32[16,4,64,256]{3,2,1,0:T(8,128)} %multiply_add_fusion.2, f32[16,256,1,1]{1,0,2,3:T(8,128)S(1)} %dynamic-slice_bitcast_fusion.9), kind=kOutput, calls=%fused_computation.5.clone.1 | convolution fusion | flops 12582912 | bytes 4227072 | tf_op jit(solution)/shard_map/while/body/eval_jaxpr/bhpn,bn->bhp/dot_general | solution.py:134
  234.8 7.2 %fusion.55 = f32[16,1,4,64]{3,1,2,0:T(1,128)S(1)} fusion(f32[16,4,64,256]{3,2,1,0:T(8,128)} %multiply_add_fusion.2, f32[16,256,1,1]{1,0,2,3:T(8,128)S(1)} %dynamic-slice_bitcast_fusion.9), kind=kOutput, calls=%fused_computation.5.clone.1 | convolution fusion | flops 12582912 | bytes 4227072 | tf_op jit(solution)/shard_map/while/body/eval_jaxpr/bhpn,bn->bhp/dot_general | solution.py:134
  246.3 7.2 %fusion.55 = f32[16,1,4,64]{3,1,2,0:T(1,128)S(1)} fusion(f32[16,4,64,256]{3,2,1,0:T(8,128)} %multiply_add_fusion.2, f32[16,256,1,1]{1,0,2,3:T(8,128)S(1)} %dynamic-slice_bitcast_fusion.9), kind=kOutput, calls=%fused_computation.5.clone.1 | convolution fusion | flops 12582912 | bytes 4227072 | tf_op jit(solution)/shard_map/while/body/eval_jaxpr/bhpn,bn->bhp/dot_general | solution.py:134
  257.8 7.2 %fusion.55 = f32[16,1,4,64]{3,1,2,0:T(1,128)S(1)} fusion(f32[16,4,64,256]{3,2,1,0:T(8,128)} %multiply_add_fusion.2, f32[16,256,1,1]{1,0,2,3:T(8,128)S(1)} %dynamic-slice_bitcast_fusion.9), kind=kOutput, calls=%fused_computation.5.clone.1 | convolution fusion | flops 12582912 | bytes 4227072 | tf_op jit(solution)/shard_map/while/body/eval_jaxpr/bhpn,bn->bhp/dot_general | solution.py:134
  269.3 7.2 %fusion.55 = f32[16,1,4,64]{3,1,2,0:T(1,128)S(1)} fusion(f32[16,4,64,256]{3,2,1,0:T(8,128)} %multiply_add_fusion.2, f32[16,256,1,1]{1,0,2,3:T(8,128)S(1)} %dynamic-slice_bitcast_fusion.9), kind=kOutput, calls=%fused_computation.5.clone.1 | convolution fusion | flops 12582912 | bytes 4227072 | tf_op jit(solution)/shard_map/while/body/eval_jaxpr/bhpn,bn->bhp/dot_general | solution.py:134
  280.8 7.2 %fusion.55 = f32[16,1,4,64]{3,1,2,0:T(1,128)S(1)} fusion(f32[16,4,64,256]{3,2,1,0:T(8,128)} %multiply_add_fusion.2, f32[16,256,1,1]{1,0,2,3:T(8,128)S(1)} %dynamic-slice_bitcast_fusion.9), kind=kOutput, calls=%fused_computation.5.clone.1 | convolution fusion | flops 12582912 | bytes 4227072 | tf_op jit(solution)/shard_map/while/body/eval_jaxpr/bhpn,bn->bhp/dot_general | solution.py:134
  292.3 7.2 %fusion.55 = f32[16,1,4,64]{3,1,2,0:T(1,128)S(1)} fusion(f32[16,4,64,256]{3,2,1,0:T(8,128)} %multiply_add_fusion.2, f32[16,256,1,1]{1,0,2,3:T(8,128)S(1)} %dynamic-slice_bitcast_fusion.9), kind=kOutput, calls=%fused_computation.5.clone.1 | convolution fusion | flops 12582912 | bytes 4227072 | tf_op jit(solution)/shard_map/while/body/eval_jaxpr/bhpn,bn->bhp/dot_general | solution.py:134
  303.8 7.2 %fusion.55 = f32[16,1,4,64]{3,1,2,0:T(1,128)S(1)} fusion(f32[16,4,64,256]{3,2,1,0:T(8,128)} %multiply_add_fusion.2, f32[16,256,1,1]{1,0,2,3:T(8,128)S(1)} %dynamic-slice_bitcast_fusion.9), kind=kOutput, calls=%fused_computation.5.clone.1 | convolution fusion | flops 12582912 | bytes 4227072 | tf_op jit(solution)/shard_map/while/body/eval_jaxpr/bhpn,bn->bhp/dot_general | solution.py:134
  315.3 7.2 %fusion.55 = f32[16,1,4,64]{3,1,2,0:T(1,128)S(1)} fusion(f32[16,4,64,256]{3,2,1,0:T(8,128)} %multiply_add_fusion.2, f32[16,256,1,1]{1,0,2,3:T(8,128)S(1)} %dynamic-slice_bitcast_fusion.9), kind=kOutput, calls=%fused_computation.5.clone.1 | convolution fusion | flops 12582912 | bytes 4227072 | tf_op jit(solution)/shard_map/while/body/eval_jaxpr/bhpn,bn->bhp/dot_general | solution.py:134
  326.8 7.2 %fusion.55 = f32[16,1,4,64]{3,1,2,0:T(1,128)S(1)} fusion(f32[16,4,64,256]{3,2,1,0:T(8,128)} %multiply_add_fusion.2, f32[16,256,1,1]{1,0,2,3:T(8,128)S(1)} %dynamic-slice_bitcast_fusion.9), kind=kOutput, calls=%fused_computation.5.clone.1 | convolution fusion | flops 12582912 | bytes 4227072 | tf_op jit(solution)/shard_map/while/body/eval_jaxpr/bhpn,bn->bhp/dot_general | solution.py:134
  338.4 7.2 %fusion.55 = f32[16,1,4,64]{3,1,2,0:T(1,128)S(1)} fusion(f32[16,4,64,256]{3,2,1,0:T(8,128)} %multiply_add_fusion.2, f32[16,256,1,1]{1,0,2,3:T(8,128)S(1)} %dynamic-slice_bitcast_fusion.9), kind=kOutput, calls=%fused_computation.5.clone.1 | convolution fusion | flops 12582912 | bytes 4227072 | tf_op jit(solution)/shard_map/while/body/eval_jaxpr/bhpn,bn->bhp/dot_general | solution.py:134
  349.9 7.2 %fusion.55 = f32[16,1,4,64]{3,1,2,0:T(1,128)S(1)} fusion(f32[16,4,64,256]{3,2,1,0:T(8,128)} %multiply_add_fusion.2, f32[16,256,1,1]{1,0,2,3:T(8,128)S(1)} %dynamic-slice_bitcast_fusion.9), kind=kOutput, calls=%fused_computation.5.clone.1 | convolution fusion | flops 12582912 | bytes 4227072 | tf_op jit(solution)/shard_map/while/body/eval_jaxpr/bhpn,bn->bhp/dot_general | solution.py:134
  361.4 7.2 %fusion.55 = f32[16,1,4,64]{3,1,2,0:T(1,128)S(1)} fusion(f32[16,4,64,256]{3,2,1,0:T(8,128)} %multiply_add_fusion.2, f32[16,256,1,1]{1,0,2,3:T(8,128)S(1)} %dynamic-slice_bitcast_fusion.9), kind=kOutput, calls=%fused_computation.5.clone.1 | convolution fusion | flops 12582912 | bytes 4227072 | tf_op jit(solution)/shard_map/while/body/eval_jaxpr/bhpn,bn->bhp/dot_general | solution.py:134
  372.9 7.2 %fusion.55 = f32[16,1,4,64]{3,1,2,0:T(1,128)S(1)} fusion(f32[16,4,64,256]{3,2,1,0:T(8,128)} %multiply_add_fusion.2, f32[16,256,1,1]{1,0,2,3:T(8,128)S(1)} %dynamic-slice_bitcast_fusion.9), kind=kOutput, calls=%fused_computation.5.clone.1 | convolution fusion | flops 12582912 | bytes 4227072 | tf_op jit(solution)/shard_map/while/body/eval_jaxpr/bhpn,bn->bhp/dot_general | solution.py:134
  384.4 7.2 %fusion.55 = f32[16,1,4,64]{3,1,2,0:T(1,128)S(1)} fusion(f32[16,4,64,256]{3,2,1,0:T(8,128)} %multiply_add_fusion.2, f32[16,256,1,1]{1,0,2,3:T(8,128)S(1)} %dynamic-slice_bitcast_fusion.9), kind=kOutput, calls=%fused_computation.5.clone.1 | convolution fusion | flops 12582912 | bytes 4227072 | tf_op jit(solution)/shard_map/while/body/eval_jaxpr/bhpn,bn->bhp/dot_general | solution.py:134
  395.9 7.2 %fusion.55 = f32[16,1,4,64]{3,1,2,0:T(1,128)S(1)} fusion(f32[16,4,64,256]{3,2,1,0:T(8,128)} %multiply_add_fusion.2, f32[16,256,1,1]{1,0,2,3:T(8,128)S(1)} %dynamic-slice_bitcast_fusion.9), kind=kOutput, calls=%fused_computation.5.clone.1 | convolution fusion | flops 12582912 | bytes 4227072 | tf_op jit(solution)/shard_map/while/body/eval_jaxpr/bhpn,bn->bhp/dot_general | solution.py:134
  407.4 7.2 %fusion.55 = f32[16,1,4,64]{3,1,2,0:T(1,128)S(1)} fusion(f32[16,4,64,256]{3,2,1,0:T(8,128)} %multiply_add_fusion.2, f32[16,256,1,1]{1,0,2,3:T(8,128)S(1)} %dynamic-slice_bitcast_fusion.9), kind=kOutput, calls=%fused_computation.5.clone.1 | convolution fusion | flops 12582912 | bytes 4227072 | tf_op jit(solution)/shard_map/while/body/eval_jaxpr/bhpn,bn->bhp/dot_general | solution.py:134
  473.6 128.6 %psum.7 = f32[24,16,4]{1,2,0:T(4,128)S(1)} all-reduce(f32[24,16,4]{1,2,0:T(4,128)S(1)} %broadcast_select_fusion), channel_id=1, replica_groups=mesh['dom'=4,'head'=32] {'head'}, use_global_device_ids=true, to_apply=%region_4.5 | all-reduce | flops 1536 | bytes 12288 | tf_op jit(solution)/shard_map/psum | solution.py:149
  610.0 82.6 %reduce-scatter.2.cloned.1.call-done = bf16[24,16,256]{2,1,0:T(8,128)(2,1)} async-done(((bf16[24,16,8192]{2,1,0:T(8,128)(2,1)}), bf16[24,16,256]{2,1,0:T(8,128)(2,1)}) %reduce-scatter.2.cloned.1.call-update) | async-done | bytes 196624 | tf_op jit(solution)/shard_map/reduce_scatter | solution.py:159
  (282 shorter events, 203.7 us)
Async XLA Ops:
  6.5 80.7 %copy-start = (bf16[8192,64]{0,1:T(8,128)(2,1)S(1)}, bf16[8192,64]{0,1:T(8,128)(2,1)}, u32[]{:S(2)}) copy-start(bf16[8192,64]{0,1:T(8,128)(2,1)} %param.27) | copy-start | bytes 3145732
  6.5 76.3 %all-gather.6.cloned.1.call-start = ((), (), s32[]{:S(2)}) async-start(), calls=%async_computation.3 | async-start | bytes 6488064 | tf_op jit(solution)/shard_map/all_gather | solution.py:64
  7.3 143.7 %all-gather.4.cloned.1.call-start = ((), (), s32[]{:S(2)}) async-start(), calls=%async_computation.2 | async-start | bytes 10485760 | tf_op jit(solution)/shard_map/all_gather | solution.py:96
  19.2 12.0 %copy-start.14 = (f32[256]{0:T(256)S(1)}, f32[256]{0:T(256)}, u32[]{:S(2)}) copy-start(f32[256]{0:T(256)} %param.25) | copy-start | bytes 3076
  19.2 37.9 %copy-start.15 = (f32[4]{0:T(128)S(1)}, f32[4]{0:T(128)}, u32[]{:S(2)}) copy-start(f32[4]{0:T(128)} %param.34) | copy-start | bytes 52
  19.2 38.0 %copy-start.4 = (f32[16,3,256]{2,0,1:T(8,128)S(1)}, f32[16,3,256]{2,0,1:T(8,128)}, u32[]{:S(2)}) copy-start(f32[16,3,256]{2,0,1:T(8,128)} %param.23) | copy-start | bytes 147460
  19.2 50.2 %copy-start.5 = (f32[16,3,64]{2,0,1:T(8,128)S(1)}, f32[16,3,64]{2,0,1:T(8,128)}, u32[]{:S(2)}) copy-start(f32[16,3,64]{2,0,1:T(8,128)} %param.24) | copy-start | bytes 36868
  19.2 62.2 %copy-start.11 = (s32[64]{0:T(128)S(1)}, s32[64]{0:T(128)}, u32[]{:S(2)}) copy-start(s32[64]{0:T(128)} %param.21) | copy-start | bytes 772
  19.2 63.5 %copy-start.8 = (f32[4,64]{1,0:T(4,128)S(1)}, f32[4,64]{1,0:T(4,128)}, u32[]{:S(2)}) copy-start(f32[4,64]{1,0:T(4,128)} %param.31) | copy-start | bytes 3076
  19.2 63.5 %copy-start.6 = (f32[4,256]{1,0:T(4,128)S(1)}, f32[4,256]{1,0:T(4,128)}, u32[]{:S(2)}) copy-start(f32[4,256]{1,0:T(4,128)} %param.29) | copy-start | bytes 12292
  82.9 4.7 copy-start.2
  87.6 1.9 copy-start.10
  98.2 77.7 %all-to-all-start = ((bf16[32,2,12288]{2,1,0:T(2,128)(2,1)}), bf16[32,2,12288]{2,1,0:T(2,128)(2,1)S(1)}, u32[]{:S(2)}, u32[]{:S(2)}) async-start(bf16[32,2,12288]{2,1,0:T(2,128)(2,1)} %reshape.155), calls=%async_computation | async-start | bytes 3145728 | tf_op jit(solution)/shard_map/all_to_all | solution.py:113
  103.9 588.8 %reduce-scatter.2.cloned.1.call-start = ((), (), s32[]{:S(2)}) async-start(), calls=%async_computation.4 | async-start | bytes 6488064 | tf_op jit(solution)/shard_map/reduce_scatter | solution.py:159
  104.1 8.3 %copy-start.9 = (f32[256]{0:T(256)S(1)}, f32[256]{0:T(256)}, u32[]{:S(2)}) copy-start(f32[256]{0:T(256)} %param.30) | copy-start | bytes 3076
  104.1 10.6 %copy-start.13 = (bf16[8192,4]{0,1:T(4,128)(2,1)S(1)}, bf16[8192,4]{0,1:T(4,128)(2,1)}, u32[]{:S(2)}) copy-start(bf16[8192,4]{0,1:T(4,128)(2,1)} %param.28) | copy-start | bytes 196612
  104.1 10.6 %copy-start.16 = (f32[4]{0:T(128)S(1)}, f32[4]{0:T(128)}, u32[]{:S(2)}) copy-start(f32[4]{0:T(128)} %param.33) | copy-start | bytes 52
  188.2 7.7 %copy-start.3 = (f32[24,16,4,64]{3,2,1,0:T(4,128)S(1)}, f32[24,16,4,64]{3,2,1,0:T(4,128)}, u32[]{:S(2)}) copy-start(f32[24,16,4,64]{3,2,1,0:T(4,128)} %custom-call.6) | copy-start | bytes 1179652
  195.9 276.3 %copy-start.12 = (f32[4]{0:T(128)S(1)}, f32[4]{0:T(128)}, u32[]{:S(2)}) copy-start(f32[4]{0:T(128)} %param.35) | copy-start | bytes 52
  195.9 407.4 %copy-start.7 = (f32[256]{0:T(256)S(1)}, f32[256]{0:T(256)}, u32[]{:S(2)}) copy-start(f32[256]{0:T(256)} %param.36) | copy-start | bytes 3076
  603.2 89.4 %copy-start.1 = (bf16[8192,64]{0,1:T(8,128)(2,1)S(1)}, bf16[8192,64]{0,1:T(8,128)(2,1)}, u32[]{:S(2)}) copy-start(bf16[8192,64]{0,1:T(8,128)(2,1)} %param.27) | copy-start | bytes 3145732
Sparse Core Ops, SparseCore 0:
  9.5 57.0 all-gather.5
  68.3 82.6 all-gather.3
  610.1 82.4 reduce-scatter.1
